TPU v7x, 512 devices: a whole 4x8x8 slice. The times are simulated.
512 devices in a mesh: ctx: 32 (over y, x), img: 16 (over z, core).
Axes of the slice: x: 4, y: 8, z: 8, core: 2. Of those that a mesh axis runs over, the one named last changes fastest.
Arguments:
- text: bfloat16 [4096, 4096], P('ctx'), may hold values from -6 to 6
- input_gain: float32 [4096], replicated, may hold values from 0.5 to 2
- q_weight: bfloat16 [4096, 4096], P('ctx', 'img'), may hold values from -0.09375 to 0.09375
- kv_weight: bfloat16 [4096, 2048], P('ctx'), may hold values from -0.09375 to 0.09375
- o_weight: bfloat16 [4096, 4096], P('img', 'ctx'), may hold values from -0.5 to 0.5
- q_gain: float32 [128], replicated, may hold values from 0.5 to 12, as said below
- k_gain: float32 [128], replicated, may hold values from 0.5 to 12, as said below
- attn_gate: float32 [1], replicated, may hold values from 0.3 to 1.5
- vision: bfloat16 [32, 256, 4096], P('img', 'ctx'), may hold values from -6 to 6
- segment_ids: int32 [4096], P('ctx'), may hold values from 0 to 127, as said below
- seg_images: int32 [128, 2], replicated, may hold values from 0 to 31, as said below
- image_slot: int32 [32], replicated, may hold values from 0 to 31, each once
Outputs:
- mixed: bfloat16 [4096, 4096], P('ctx', 'img')
Inputs may be any that keep to these rules, and one draw needn't show every extreme that they name: `segment_ids`: numbers never fall along the tokens; block c of 128 tokens uses numbers from c * 4 on, 1 to 4 segments a block, and some block has 4. `seg_images`: each row names 2 different images; the tokens of one block of 128 see at most 8 different images, and some block sees exactly 8. `image_slot`: A permutation. `q_gain`: Positive. `k_gain`: Positive.
All inputs are finite; a program needn't handle non-finite values.
Results may differ from a plain program's by a relative error of at most 0.022.
The roundings to bfloat16 on the way count: a program that leaves them out, or rounds other values in their place, can miss the bound.
Values may be sent and summed in bfloat16 or wider, within the bound.
A program may use at most 64 MiB of HBM per device.

v0:
```python
import jax
import jax.numpy as jnp
from jax import lax
from jax.sharding import PartitionSpec as P

KVH = 8


EPS = 1e-05
NEG = -1e30


def head_norm(values, gain):
    mean_sq = jnp.mean(values * values, axis=-1, keepdims=True)
    return values * lax.rsqrt(mean_sq + EPS) * gain


def attend(query, keys, values, mask, carry):
    top, total, acc = carry
    scale = query.shape[-1] ** (-0.5)
    scores = jnp.einsum("tkgd,nkd->tkgn", query, keys, preferred_element_type=jnp.float32) * scale
    live = mask[:, None, None, :]
    scores = jnp.where(live, scores, NEG)
    fresh = jnp.maximum(top, jnp.max(scores, axis=-1))
    weights = jnp.where(live, jnp.exp(scores - fresh[..., None]), 0.0)
    total = jnp.sum(weights, axis=-1)
    acc = jnp.einsum(
        "tkgn,nkd->tkgd", weights.astype(jnp.bfloat16), values, preferred_element_type=jnp.float32
    )
    return (fresh, total, acc)


def body(
    text,
    input_gain,
    q_weight,
    kv_weight,
    o_weight,
    q_gain,
    k_gain,
    attn_gate,
    vision,
    segment_ids,
    seg_images,
    image_slot,
):
    tokens_here = text.shape[0]
    head_dim = q_gain.shape[0]
    hidden = head_norm(text.astype(jnp.float32), input_gain).astype(jnp.bfloat16)
    query = jnp.dot(
        hidden,
        lax.all_gather(q_weight, "ctx", axis=0, tiled=True),
        preferred_element_type=jnp.float32,
    )
    heads_here = q_weight.shape[1] // head_dim
    img_count = lax.axis_size("img")
    kv_heads = max(1, KVH // img_count)
    group = heads_here // kv_heads
    query = head_norm(query.reshape(tokens_here, kv_heads, group, head_dim), q_gain).astype(
        jnp.bfloat16
    )
    first_head = lax.axis_index("img") * KVH // img_count
    own_columns = lax.dynamic_slice_in_dim(
        kv_weight, first_head * 2 * head_dim, kv_heads * 2 * head_dim, 1
    )
    kv_columns = lax.all_gather(own_columns, "ctx", axis=0, tiled=True)
    projected = jnp.einsum(
        "ntd,dc->ntc",
        lax.all_gather(vision, "img", axis=0, tiled=True),
        kv_columns,
        preferred_element_type=jnp.float32,
    )
    images = projected.shape[0]
    vt_dev = projected.shape[1]
    paired = projected.reshape(images, vt_dev, kv_heads, 2, head_dim)
    keys = head_norm(paired[:, :, :, 0], k_gain).astype(jnp.bfloat16)
    values = paired[:, :, :, 1].astype(jnp.bfloat16)
    kv_block = jnp.stack((keys, values), axis=3)
    own_slots = jnp.take(image_slot, jnp.take(seg_images, segment_ids, axis=0), axis=0)
    slot_ids = jnp.arange(images, dtype=jnp.int32)
    sees = jnp.any(own_slots[:, :, None] == slot_ids[None, None, :], axis=1)
    init = (
        jnp.full((tokens_here, kv_heads, group), NEG, jnp.float32),
        jnp.zeros((tokens_here, kv_heads, group), jnp.float32),
        jnp.zeros((tokens_here, kv_heads, group, head_dim), jnp.float32),
    )
    piece = lax.all_gather(kv_block, "ctx", axis=1, tiled=True)
    rows = piece.shape[1]
    flat = piece.reshape(images * rows, kv_heads, 2, head_dim)
    mask = jnp.repeat(sees, rows, axis=1)
    top, total, acc = attend(query, flat[:, :, 0], flat[:, :, 1], mask, init)
    context = (
        (acc / total[..., None]).astype(jnp.bfloat16).reshape(tokens_here, heads_here * head_dim)
    )
    partial_terms = jnp.dot(
        context,
        lax.all_gather(o_weight, "ctx", axis=1, tiled=True),
        preferred_element_type=jnp.float32,
    )
    update = lax.psum_scatter(
        partial_terms.astype(jnp.bfloat16), "img", scatter_dimension=1, tiled=True
    ).astype(jnp.float32)
    own_width = update.shape[1]
    own_text = lax.dynamic_slice_in_dim(text, lax.axis_index("img") * own_width, own_width, 1)
    return (own_text.astype(jnp.float32) + jnp.tanh(attn_gate[0]) * update).astype(jnp.bfloat16)


def solution(mesh):
    return jax.shard_map(
        body,
        mesh=mesh,
        in_specs=(
            P("ctx", None),
            P(),
            P("ctx", "img"),
            P("ctx", None),
            P("img", "ctx"),
            P(),
            P(),
            P(),
            P("img", "ctx", None),
            P("ctx"),
            P(),
            P(),
        ),
        out_specs=P("ctx", "img"),
        check_vma=False,
    )
```

profile of v0, /device:TPU:1, one launch (start us, length us, event | category | flops | bytes accessed | tf_op | source)
XLA Modules:
  0.0 463.8 jit_solution(11100508908342649206)
XLA Ops:
  6.5 0.0 copy-start
  6.5 0.0 all-gather.8.cloned.1.call-start
  6.5 0.7 all-gather.8.cloned.1.call-update
  7.3 0.0 all-gather.6.cloned.1.call-start
  7.3 0.3 copy-done
  7.6 0.6 constant_dynamic-slice_fusion
  8.2 0.0 all-gather.6.cloned.1.call-update
  8.2 0.0 all-gather.12.cloned.1.call-start
  8.3 0.7 all-gather.12.cloned.1.call-update
  9.0 0.0 copy-start.4
  9.0 0.0 copy-start.6
  9.0 0.0 copy-start.3
  9.0 0.0 all-gather.10.cloned.1.call-start
  9.1 49.5 %all-gather.8.cloned.1.call-done = bf16[32,8,4096]{2,1,0:T(8,128)(2,1)} async-done(((bf16[2,8,4096]{2,1,0:T(8,128)(2,1)}), bf16[32,8,4096]{2,1,0:T(8,128)(2,1)}) %all-gather.8.cloned.1.call-update) | async-done | bytes 2097168 | tf_op jit(solution)/shard_map/all_gather | solution.py:69
  58.6 80.4 %all-gather.6.cloned.1.call-done = bf16[4096,256]{1,0:T(8,128)(2,1)} async-done(((bf16[128,256]{1,0:T(8,128)(2,1)}), bf16[4096,256]{1,0:T(8,128)(2,1)}) %all-gather.6.cloned.1.call-update) | async-done | bytes 2097168 | tf_op jit(solution)/shard_map/all_gather | solution.py:66
  139.0 3.7 fusion.16
  142.7 0.0 copy-start.1
  142.7 0.1 reshape.202
  142.9 0.1 slice.21
  143.0 0.1 slice.22
  143.1 0.1 multiply_reduce_fusion
  143.3 0.0 copy-done.4
  143.3 0.1 multiply_convert_fusion
  143.4 0.7 pad_maximum_fusion
  144.0 0.0 all-gather.10.cloned.1.call-update
  144.1 0.0 all-gather.14.cloned.1.call-start
  144.1 0.5 all-gather.14.cloned.1.call-update
  144.6 0.0 reduce-scatter.2.cloned.1.call-start
  144.7 0.0 copy-done.6
  144.7 0.0 copy-done.3
  144.7 0.1 copy.56
  144.9 0.6 gather_fusion
  145.5 0.1 compare_select_fusion
  145.6 0.1 reshape.218
  145.7 0.0 copy-done.1
  145.8 0.0 copy-start.2
  145.8 0.0 copy-start.7
  145.8 0.0 copy-start.5
  145.8 1.9 gather_fusion.1
  147.7 0.1 reshape.217
  147.8 0.1 and_select_fusion
  147.9 0.1 copy.57
  148.0 0.0 copy-done.2
  148.0 0.3 fusion.10
  148.3 0.0 copy-done.7
  148.3 74.6 %all-gather.12.cloned.1.call-done = bf16[4096,256]{1,0:T(8,128)(2,1)} async-done(((bf16[128,256]{1,0:T(8,128)(2,1)}), bf16[4096,256]{1,0:T(8,128)(2,1)}) %all-gather.12.cloned.1.call-update) | async-done | bytes 2097168 | tf_op jit(solution)/shard_map/all_gather | solution.py:52
  222.9 0.0 copy-done.5
  222.9 2.1 fusion.41
  225.0 0.1 mul.140
  225.1 0.2 reduce_sum.38
  225.3 86.3 %all-gather.10.cloned.1.call-done = bf16[32,256,1,2,128]{4,0,3,2,1:T(8,128)(2,1)} async-done(((bf16[32,8,1,2,128]{4,0,3,2,1:T(8,128)(2,1)}), bf16[32,256,1,2,128]{4,0,3,2,1:T(8,128)(2,1)}) %all-gather.10.cloned.1.call-update) | async-done | bytes 4194320 | tf_op jit(solution)/shard_map/all_gather | solution.py:87
  311.6 4.9 %copy.55 = bf16[32,256,1,2,128]{4,1,0,3,2:T(8,128)(2,1)S(1)} copy(bf16[32,256,1,2,128]{4,0,3,2,1:T(8,128)(2,1)} %all-gather.10.cloned.1.call-done) | data formatting | bytes 8388608 | tf_op jit(solution)/shard_map/all_gather | solution.py:87
  316.5 0.3 broadcast_in_dim.61
  316.8 0.2 mul.141
  317.0 1.8 fusion.42
  318.8 1.7 fusion.2
  320.5 1.7 fusion.27
  322.2 69.7 %all-gather.14.cloned.1.call-done = bf16[256,4096]{1,0:T(8,128)(2,1)} async-done(((bf16[256,128]{1,0:T(8,128)(2,1)}), bf16[256,4096]{1,0:T(8,128)(2,1)}) %all-gather.14.cloned.1.call-update) | async-done | bytes 2097168 | tf_op jit(solution)/shard_map/all_gather | solution.py:97
  391.9 3.0 convolution_convert_fusion
  394.9 0.0 reduce-scatter.2.cloned.1.call-update
  395.6 59.8 %reduce-scatter.2.cloned.1.call-done = bf16[128,256]{1,0:T(8,128)(2,1)} async-done(((bf16[128,4096]{1,0:T(8,128)(2,1)}), bf16[128,256]{1,0:T(8,128)(2,1)}) %reduce-scatter.2.cloned.1.call-update) | async-done | bytes 65552 | tf_op jit(solution)/shard_map/reduce_scatter | solution.py:100
  455.5 1.5 add_convert_fusion
  (11 shorter events, 0.1 us)
Async XLA Ops:
  6.5 1.0 copy-start
  6.5 52.1 %all-gather.8.cloned.1.call-start = ((), (), s32[]{:S(2)}) async-start(), calls=%async_computation.2 | async-start | bytes 2228224 | tf_op jit(solution)/shard_map/all_gather | solution.py:69
  7.3 131.7 %all-gather.6.cloned.1.call-start = ((), (), s32[]{:S(2)}) async-start(), calls=%async_computation.1 | async-start | bytes 2162688 | tf_op jit(solution)/shard_map/all_gather | solution.py:66
  8.2 214.7 %all-gather.12.cloned.1.call-start = ((), (), s32[]{:S(2)}) async-start(), calls=%async_computation.4 | async-start | bytes 2162688 | tf_op jit(solution)/shard_map/all_gather | solution.py:52
  9.0 134.3 %copy-start.4 = (f32[128]{0:T(128)S(1)}, f32[128]{0:T(128)}, u32[]{:S(2)}) copy-start(f32[128]{0:T(128)} %param.18) | copy-start | bytes 1540
  9.0 135.7 %copy-start.6 = (s32[128]{0:T(128)S(1)}, s32[128]{0:T(128)}, u32[]{:S(2)}) copy-start(s32[128]{0:T(128)} %param.21) | copy-start | bytes 1540
  9.0 135.7 %copy-start.3 = (s32[128,2]{0,1:T(2,128)S(1)}, s32[128,2]{0,1:T(2,128)}, u32[]{:S(2)}) copy-start(s32[128,2]{0,1:T(2,128)} %param.22) | copy-start | bytes 3076
  9.0 302.6 %all-gather.10.cloned.1.call-start = ((), (), s32[]{:S(2)}) async-start(), calls=%async_computation.3 | async-start | bytes 4325376 | tf_op jit(solution)/shard_map/all_gather | solution.py:87
  142.7 3.1 copy-start.1
  144.1 247.8 %all-gather.14.cloned.1.call-start = ((), (), s32[]{:S(2)}) async-start(), calls=%async_computation.5 | async-start | bytes 2162688 | tf_op jit(solution)/shard_map/all_gather | solution.py:97
  144.6 310.8 %reduce-scatter.2.cloned.1.call-start = ((), (), s32[]{:S(2)}) async-start(), calls=%async_computation.6 | async-start | bytes 1114112 | tf_op jit(solution)/shard_map/reduce_scatter | solution.py:100
  145.8 2.2 copy-start.2
  145.8 2.5 copy-start.7
  145.8 77.2 %copy-start.5 = (f32[4096]{0:T(1024)S(1)}, f32[4096]{0:T(1024)}, u32[]{:S(2)}) copy-start(f32[4096]{0:T(1024)} %param.13) | copy-start | bytes 49156
Sparse Core Ops, SparseCore 0:
  9.5 49.0 all-gather.7
  61.8 77.1 all-gather.5
  142.2 80.7 all-gather.11
  226.0 85.6 all-gather.9
  314.5 77.3 all-gather.13
  395.1 60.3 reduce-scatter.1
where the time goes:
time: 466 us; the launch traced here: 464 us
  waiting for transfers between devices  422 us (91%)
  between operations  14.5 us (3%)
  matrix products  12.3 us (3%)
  local copies, waits for them, and re-layouts  9.71 us (2%)
  other arithmetic  4.78 us (1%)
    all_gather x1, waiting for transfers between devices, body(): piece = lax.all_gather(kv_block, 'ctx', axis=1, tiled=True)  86.3 us
    all_gather x1, waiting for transfers between devices, body(): kv_columns = lax.all_gather(own_columns, 'ctx', axis=0, tiled=True)  80.4 us
    all_gather x1, waiting for transfers between devices, body(): lax.all_gather(q_weight, 'ctx', axis=0, tiled=True)  74.6 us
    all_gather x1, waiting for transfers between devices, body(): lax.all_gather(o_weight, 'ctx', axis=1, tiled=True)  69.7 us
    reduce_scatter x1, waiting for transfers between devices, body(): lax.psum_scatter(partial_terms.astype(jnp.bfloat16), 'img', scatter_dimen...  59.8 us
    all_gather x1, waiting for transfers between devices, body(): lax.all_gather(vision, 'img', axis=0, tiled=True)  49.5 us
  transfers between devices with their start and end apart: 6, of which 6 were waited for; matrix products, arithmetic and copies ran while one was open for 5% of the time, Pallas kernels for 0%

commit v1 on v0

v1 whole, which is shorter than its diff:
```python
import functools

import jax
import jax.numpy as jnp
from jax import lax
from jax.experimental import pallas as pl
from jax.experimental.pallas import tpu as pltpu
from jax.sharding import PartitionSpec as P

MESH = pl.DeviceIdType.MESH
EPS = 1e-05
NEG = -1e30
F32 = jnp.float32
BF16 = jnp.bfloat16
NX, NY, NZ = 4, 8, 8
COPIES = 192


def kernel(
    text_ref, in_gain_ref, qw_ref, kvw_ref, ow_ref, q_gain_ref, k_gain_ref, gate_ref, vis_ref,
    seg_ref, seg_img_ref, slot_ref, out_ref,
    text, hid, hid_in, vis, wkv, wq, wo, wo_other, part, part_in, kv_rows, stage, kv_all, ctx, upd, upd_in,
    send_sem, recv_sem, local_sem,
):
    c = lax.axis_index("ctx")
    i = lax.axis_index("img")
    x, y, z, k = lax.rem(c, NX), c // NX, i // 2, lax.rem(i, 2)
    wrap = lambda a, n: lax.rem(a + 2 * n, n)
    at = lambda xx, yy, zz, kk: (yy * NX + xx, zz * 2 + kk)
    to_x = lambda d: at(wrap(x + d, NX), y, z, k)
    to_y = lambda d: at(x, wrap(y + d, NY), z, k)
    to_z = lambda d: at(x, y, wrap(z + d, NZ), k)
    other = at(x, y, z, 1 - k)
    sent = []

    def send(src, dst, device):
        n = len(sent)
        copy = pltpu.make_async_remote_copy(
            src_ref=src, dst_ref=dst, send_sem=send_sem.at[n], recv_sem=recv_sem.at[n],
            device_id=device, device_id_type=MESH,
        )
        copy.start()
        sent.append(copy)
        return copy

    barrier = pltpu.get_barrier_semaphore()
    peers = [to_x(d) for d in (1, 2, 3)] + [to_y(d) for d in range(1, NY)]
    peers += [to_z(d) for d in range(1, NZ)] + [other]
    for peer in peers:
        pl.semaphore_signal(barrier, inc=1, device_id=peer, device_id_type=MESH)
    local = []

    def fetch(src, dst):
        copy = pltpu.make_async_copy(src, dst, local_sem.at[len(local)])
        copy.start()
        local.append(copy)
        return copy

    get_text = fetch(text_ref, text)
    get_own = [
        fetch(vis_ref.at[:, pl.ds(0, 2048)], vis.at[z, k, 0]),
        fetch(vis_ref.at[:, pl.ds(2048, 2048)], vis.at[z, k, 1]),
        fetch(kvw_ref.at[:, pl.ds(pl.multiple_of(z * 256 + k * 128, 128), 128)], wkv.at[c]),
        fetch(qw_ref, wq.at[y]),
        fetch(ow_ref, wo.at[c]),
    ]
    get_text.wait()

    @pl.loop(0, 8)
    def _(block):
        rows = pl.ds(pl.multiple_of(block * 16, 16), 16)
        values = text[rows, :].astype(F32)
        mean_sq = jnp.mean(values * values, axis=-1, keepdims=True)
        values = (values * lax.rsqrt(mean_sq + EPS) * in_gain_ref[...]).astype(BF16)
        for b in range(32):
            hid[b % NX, b // NX // 4, b // NX % 4, rows, :] = values[:, b * 128:(b + 1) * 128]

    for copy in get_own:
        copy.wait()
    pl.semaphore_wait(barrier, len(peers))

    vis_p, vis_m, vis_o = {}, {}, []
    for h in (0, 1):
        vis_p[1, h] = send(vis.at[z, k, h], vis.at[z, k, h], to_z(1))
        vis_m[1, h] = send(vis.at[z, k, h], vis.at[z, k, h], to_z(-1))
    kv_y = {d: send(wkv.at[c], wkv.at[c], to_y(d)) for d in (1, -1, 2, -2, 3, -3, 4)}
    kv_x = [send(wkv.at[c], wkv.at[c], to_x(d)) for d in (1, -1, 2)]
    for h in (0, 1):
        vis_o.append(send(vis.at[z, k, h], vis.at[z, k, h], other))
    q_p, q_m = {}, {}
    q_p[1] = send(wq.at[y], wq.at[y], to_y(1))
    q_m[1] = send(wq.at[y], wq.at[y], to_y(-1))
    hid_x = {}
    for d in (1, 3, 2):
        hid_x[d] = send(hid.at[wrap(x + d, NX), k], hid_in.at[d - 1, k], to_x(d))
    o_xp = send(wo.at[c], wo.at[c], to_x(1))
    o_xm = send(wo.at[c], wo.at[c], to_x(-1))

    def vis_step(s):
        for h in (0, 1):
            for ring, sign in ((vis_p, 1), (vis_m, -1)):
                if (s, h) not in ring:
                    continue
                ring[s, h].wait_recv()
                block = vis.at[wrap(z - sign * s, NZ), k, h]
                if s < 3 or (s == 3 and h == (0 if sign == 1 else 1)):
                    ring[s + 1, h] = send(block, block, to_z(sign))
                vis_o.append(send(block, block, other))

    def kv_step(s):
        for d in ((s, -s) if s < 4 else (4,)):
            kv_y[d].wait_recv()
            block = wkv.at[wrap(y - d, NY) * NX + x]
            for e in (1, -1, 2):
                kv_x.append(send(block, block, to_x(e)))

    def q_step(s):
        for ring, sign in ((q_p, 1), (q_m, -1)):
            ring[s].wait_recv()
            block = wq.at[wrap(y - sign * s, NY)]
            if s == 3:
                block = block.at[pl.ds(0 if sign == 1 else 64, 64)]
            if s < 4:
                ring[s + 1] = send(block, block, to_y(sign))

    o_p, o_m = {}, {}

    def o_bundle(yy, first=0, count=NX):
        return wo.at[pl.ds(yy * NX + first, count)]

    def o_step(s):
        for ring, sign in ((o_p, 1), (o_m, -1)):
            ring[s].wait_recv()
            yy = wrap(y - sign * s, NY)
            block = o_bundle(yy)
            if s == 3:
                block = o_bundle(yy, 0 if sign == 1 else 2, 2)
            if s < 4:
                ring[s + 1] = send(block, block, to_y(sign))
                o_share(yy)
        if s == 4:
            o_share(wrap(y + 4, NY))

    o_o = []

    def o_share(yy):
        o_o.append(send(wo.at[pl.ds(yy * NX + 2 * (1 - k), 2)], wo_other.at[yy], other))

    vis_step(1)
    kv_step(1)
    vis_step(2)
    kv_step(2)
    q_step(1)
    o_xp.wait_recv()
    o_xm.wait_recv()
    half = wo.at[y * NX + wrap(x - 1, NX), pl.ds(0, 128)]
    o_x2p = send(half, half, to_x(1))
    half = wo.at[y * NX + wrap(x + 1, NX), pl.ds(128, 128)]
    o_x2m = send(half, half, to_x(-1))
    kv_step(3)
    kv_step(4)
    vis_step(3)
    q_step(2)
    hid_o = {}
    for d in (1, 3, 2):
        hid_x[d].wait_recv()
        hid_o[d] = send(hid_in.at[d - 1, k], hid_in.at[d - 1, k], other)
    vis_step(4)
    q_step(3)
    for copy in kv_x:
        copy.wait_recv()
    for copy in vis_o:
        copy.wait_recv()

    rows = jnp.zeros((256, 128), F32)
    for h in (0, 1):
        rows += jnp.dot(
            vis[:, :, h].reshape(256, 2048), wkv[16 * h:16 * (h + 1)].reshape(2048, 128),
            preferred_element_type=F32,
        )
    mean_sq = jnp.mean(rows * rows, axis=-1, keepdims=True)
    normed = rows * lax.rsqrt(mean_sq + EPS) * k_gain_ref[...]
    kv_rows[...] = jnp.where(k == 0, normed, rows).reshape(32, 8, 128)

    offsets = [(dx, dy) for dy in (0, 4, 3, 5, 2, 6, 1, 7) for dx in (2, 1, 3, 0)]

    def pick(block):
        tiles = []
        for s in range(8):
            slot = slot_ref[seg_img_ref[block * 8 + s]]
            tiles.append(kv_rows[slot])
        return jnp.concatenate(tiles, axis=0).astype(BF16)

    kv_a = {}
    kv_all[k, 0] = pick(c)
    for dx, dy in offsets:
        if (dx, dy) == (0, 0):
            continue
        n = dy * NX + dx
        xx, yy = wrap(x + dx, NX), wrap(y + dy, NY)
        stage[n] = pick(yy * NX + xx)
        kv_a[n] = send(stage.at[n], kv_all.at[k, n], at(xx, yy, z, k))

    o_x2p.wait_recv()
    o_x2m.wait_recv()
    o_p[1] = send(o_bundle(y), o_bundle(y), to_y(1))
    o_m[1] = send(o_bundle(y), o_bundle(y), to_y(-1))
    o_share(y)
    q_step(4)
    for copy in hid_o.values():
        copy.wait_recv()
    wq_all = wq[...].reshape(1024, 256)
    part_x = {}
    query = None
    for d in (1, 3, 2, 0):
        blocks = [
            (hid[x, b // 4, b % 4] if d == 0 else hid_in[d - 1, b // 4, b % 4]) for b in range(8)
        ]
        product = jnp.dot(jnp.concatenate(blocks, axis=1), wq_all, preferred_element_type=F32)
        if d == 0:
            query = product
        else:
            part[d - 1] = product.astype(BF16)
            part_x[d] = send(part.at[d - 1], part_in.at[d - 1], to_x(-d))
    o_step(1)
    for d in (1, 3, 2):
        part_x[d].wait_recv()
        query += part_in[d - 1].astype(F32)
    heads = []
    for n in (0, 1):
        head = query[:, 128 * n:128 * (n + 1)]
        mean_sq = jnp.mean(head * head, axis=-1, keepdims=True)
        heads.append((head * lax.rsqrt(mean_sq + EPS) * q_gain_ref[...]).astype(BF16))

    kv_o = []
    for dy in (1, 7, 2, 6, 3, 5, 4, 0):
        for dx in range(NX):
            if (dx, dy) != (0, 0):
                kv_a[dy * NX + dx].wait_recv()
        block = kv_all.at[k, pl.ds(dy * NX, NX)]
        kv_o.append(send(block, block, other))
    o_step(2)
    for copy in kv_o:
        copy.wait_recv()

    keys = kv_all[0].reshape(2048, 128)
    values = kv_all[1].reshape(2048, 128)
    column = lax.broadcasted_iota(jnp.int32, (128, 2048), 1)
    live = lax.rem(column, 64) // 16 == seg_ref[...] - 4 * c
    for n in (0, 1):
        scores = lax.dot_general(
            heads[n], keys, (((1,), (1,)), ((), ())), preferred_element_type=F32
        ) * (128 ** -0.5)
        scores = jnp.where(live, scores, NEG)
        weights = jnp.exp(scores - jnp.max(scores, axis=-1, keepdims=True))
        total = jnp.sum(weights, axis=-1, keepdims=True)
        acc = jnp.dot(weights.astype(BF16), values, preferred_element_type=F32)
        ctx[k, :, 128 * n:128 * (n + 1)] = (acc / total).astype(BF16)
    ctx_o = send(ctx.at[k], ctx.at[k], other)
    o_step(3)
    o_step(4)
    for copy in o_o:
        copy.wait_recv()
    ctx_o.wait_recv()

    upd_z = {}
    mine, theirs = ctx[k], ctx[1 - k]
    update = None
    for d in (4, 3, 5, 2, 6, 1, 7, 0):
        zz = wrap(z + d, NZ)
        own_w = jnp.concatenate([wo[zz * NX + 2 * k + e] for e in (0, 1)], axis=1)
        other_w = jnp.concatenate([wo_other[zz, e] for e in (0, 1)], axis=1)
        product = jnp.dot(mine, own_w, preferred_element_type=F32)
        product += jnp.dot(theirs, other_w, preferred_element_type=F32)
        if d == 0:
            update = product.astype(BF16).astype(F32)
        else:
            upd[d - 1] = product.astype(BF16)
            upd_z[d] = send(upd.at[d - 1], upd_in.at[d - 1], to_z(d))
    for d in (1, 7, 2, 6, 3, 5, 4):
        upd_z[d].wait_recv()
        update += upd_in[d - 1].astype(F32)
    own_text = text[:, pl.ds(pl.multiple_of(i * 256, 256), 256)].astype(F32)
    gate = jnp.tanh(jnp.full((1, 256), gate_ref[0], F32))
    out_ref[...] = (own_text + gate * update).astype(BF16)
    for copy in sent:
        copy.wait_send()


def body(
    text, input_gain, q_weight, kv_weight, o_weight, q_gain, k_gain, attn_gate, vision, segment_ids,
    seg_images, image_slot,
):
    vmem = pl.BlockSpec(memory_space=pltpu.VMEM)
    smem = pl.BlockSpec(memory_space=pltpu.SMEM)
    hbm = pl.BlockSpec(memory_space=pl.ANY)
    return pl.pallas_call(
        kernel,
        out_shape=jax.ShapeDtypeStruct((128, 256), BF16),
        in_specs=[hbm, vmem, hbm, hbm, hbm, vmem, vmem, smem, hbm, vmem, smem, smem],
        out_specs=vmem,
        scratch_shapes=[
            pltpu.VMEM((128, 4096), BF16),
            pltpu.VMEM((4, 2, 4, 128, 128), BF16),
            pltpu.VMEM((3, 2, 4, 128, 128), BF16),
            pltpu.VMEM((8, 2, 2, 16, 2048), BF16),
            pltpu.VMEM((32, 128, 128), BF16),
            pltpu.VMEM((8, 128, 256), BF16),
            pltpu.VMEM((32, 256, 128), BF16),
            pltpu.VMEM((8, 2, 256, 128), BF16),
            pltpu.VMEM((3, 128, 256), BF16),
            pltpu.VMEM((3, 128, 256), BF16),
            pltpu.VMEM((32, 8, 128), F32),
            pltpu.VMEM((32, 64, 128), BF16),
            pltpu.VMEM((2, 32, 64, 128), BF16),
            pltpu.VMEM((2, 128, 256), BF16),
            pltpu.VMEM((7, 128, 256), BF16),
            pltpu.VMEM((7, 128, 256), BF16),
            pltpu.SemaphoreType.DMA((COPIES,)),
            pltpu.SemaphoreType.DMA((COPIES,)),
            pltpu.SemaphoreType.DMA((8,)),
        ],
        compiler_params=pltpu.CompilerParams(
            collective_id=0, has_side_effects=True, vmem_limit_bytes=48 * 2**20
        ),
        cost_estimate=pl.CostEstimate(flops=2 * 10**9, bytes_accessed=4 * 10**6, transcendentals=600000),
    )(
        text, input_gain.reshape(1, -1), q_weight, kv_weight, o_weight, q_gain.reshape(1, -1),
        k_gain.reshape(1, -1), attn_gate, vision.reshape(16, 4096), segment_ids.reshape(-1, 1),
        seg_images.reshape(-1), image_slot,
    )


def solution(mesh):
    return jax.shard_map(
        body,
        mesh=mesh,
        in_specs=(
            P("ctx", None), P(), P("ctx", "img"), P("ctx", None), P("img", "ctx"), P(), P(), P(),
            P("img", "ctx", None), P("ctx"), P(), P(),
        ),
        out_specs=P("ctx", "img"),
        check_vma=False,
    )
```

time: 466 us -> 101 us (0.22)
  waiting for transfers between devices: 422 us -> 0 us
  Pallas kernels: 0 us -> 93 us
  between operations: 14.5 us -> 0.75 us
  matrix products: 12.3 us -> 0 us
  other arithmetic: 4.78 us -> 0 us
    all_gather x5 -> x0, waiting for transfers between devices: 361 us -> none  [the longest x1 86.3 us: body(): piece = lax.all_gather(kv_block, 'ctx', axis=1, tiled=True)]
    pallas_call x0 -> x1, Pallas kernels: none -> 93 us  [body(): pl.pallas_call(kernel, out_shape=jax.ShapeDtypeStruct((128, 256), BF16),...]
    reduce_scatter x1 -> x0, waiting for transfers between devices: 59.8 us -> none  [body(): lax.psum_scatter(partial_terms.astype(jnp.bfloat16), 'img', scatter_dimen...]
    dot_general x5 -> x0, matrix products: 12.3 us -> none  [the longest x1 3.68 us: body(): jnp.einsum('ntd,dc->ntc', lax.all_gather(vision, 'img', axis=0, tiled=Tru...]
    unnamed x18 -> x20, local copies, waits for them, and re-layouts: 0.42 us -> 5.79 us
    all_gather x1 -> x0, local copies, waits for them, and re-layouts: 4.89 us -> none  [body(): piece = lax.all_gather(kv_block, 'ctx', axis=1, tiled=True)]
  transfers between devices with their start and end apart: 6 -> 0, of which waited for: 6 -> 0; matrix products, arithmetic and copies ran while one was open for 5% -> 0% of each run, Pallas kernels for 0% -> 0%
where the time goes in v1:
time: 101 us; the launch traced here: 100 us
  Pallas kernels  93 us (92%)
  local copies, waits for them, and re-layouts  6.68 us (7%)
    pallas_call x1, Pallas kernels, body(): pl.pallas_call(kernel, out_shape=jax.ShapeDtypeStruct((128, 256), BF16),...  93 us
    unnamed x20, local copies, waits for them, and re-layouts  5.79 us

profile of v1, /device:TPU:1, one launch (start us, length us, event | category | flops | bytes accessed | tf_op | source)
XLA Modules:
  0.0 100.4 jit_solution(10680528819774552508)
XLA Ops:
  0.0 0.0 copy-start.2
  0.7 0.8 copy.15.seg_ref
  1.5 0.0 copy-start.3
  1.5 0.8 copy.14
  2.3 0.0 copy-start.6
  2.3 0.0 copy-start.7
  2.3 0.0 copy-start.8
  2.3 0.1 reshape.23.seg_img_ref
  2.4 0.0 copy-done.2
  2.5 0.0 copy-done.3
  2.5 0.5 copy-done.6
  2.9 0.0 copy-done.7
  3.0 0.0 copy-done.8
  3.0 0.0 copy-start
  3.0 1.2 %copy-done = bf16[128,4096]{1,0:T(8,128)(2,1)S(1)} copy-done((bf16[128,4096]{1,0:T(8,128)(2,1)S(1)}, bf16[128,4096]{1,0:T(8,128)(2,1)}, u32[]{:S(2)}) %copy-start) | copy-done | bytes 1048600
  4.2 0.0 copy-start.1
  4.2 1.0 %copy-done.1 = bf16[128,2048]{1,0:T(8,128)(2,1)S(1)} copy-done((bf16[128,2048]{1,0:T(8,128)(2,1)S(1)}, bf16[128,2048]{1,0:T(8,128)(2,1)}, u32[]{:S(2)}) %copy-start.1) | copy-done | bytes 524312
  5.2 0.0 copy-start.4
  5.2 0.8 copy-done.4
  6.1 0.0 copy-start.5
  6.1 0.7 copy-done.5
  6.8 93.0 %shard_map.118 = bf16[128,256]{1,0:T(8,128)(2,1)S(1)} custom-call(bf16[128,4096]{1,0:T(8,128)(2,1)S(1)} %copy-done, f32[1,4096]{1,0:T(1,128)S(1)} %bitcast.6, bf16[128,256]{1,0:T(8,128)(2,1)S(1)} %copy-done.3, bf16[128,2048]{1,0:T(8,128)(2,1)S(1)} %copy-done.1, bf16[256,128]{1,0:T(8,128)(2,1)S(1)} %copy-done.4, f32[1,128]{1,0:T(1,128)S(1)} %bitcast.7, ...), custom_call_target="tpu_custom_call" | custom-call | flops 2000000000 | bytes 4000000 | tf_op jit(solution)/shard_map/pallas_call | solution.py:297
  99.8 0.6 copy.18
Async XLA Ops:
  0.0 2.4 %copy-start.2 = (bf16[2,8,4096]{2,1,0:T(8,128)(2,1)S(1)}, bf16[2,8,4096]{2,1,0:T(8,128)(2,1)}, u32[]{:S(2)}) copy-start(bf16[2,8,4096]{2,1,0:T(8,128)(2,1)} %param.20) | copy-start | bytes 393220
  1.5 1.0 %copy-start.3 = (bf16[128,256]{1,0:T(8,128)(2,1)S(1)}, bf16[128,256]{1,0:T(8,128)(2,1)}, u32[]{:S(2)}) copy-start(bf16[128,256]{1,0:T(8,128)(2,1)} %qw_ref.1) | copy-start | bytes 196612
  2.3 0.7 copy-start.6
  2.3 0.7 copy-start.7
  2.3 0.7 copy-start.8
  3.0 1.2 %copy-start = (bf16[128,4096]{1,0:T(8,128)(2,1)S(1)}, bf16[128,4096]{1,0:T(8,128)(2,1)}, u32[]{:S(2)}) copy-start(bf16[128,4096]{1,0:T(8,128)(2,1)} %text_ref.1) | copy-start | bytes 3145732
  4.2 1.0 %copy-start.1 = (bf16[128,2048]{1,0:T(8,128)(2,1)S(1)}, bf16[128,2048]{1,0:T(8,128)(2,1)}, u32[]{:S(2)}) copy-start(bf16[128,2048]{1,0:T(8,128)(2,1)} %kvw_ref.1) | copy-start | bytes 1572868
  5.2 0.8 copy-start.4
  6.1 0.7 copy-start.5

commit v2 on v1

--- a/solution.py
+++ b/solution.py
@@ -17,9 +17,9 @@
 
 
 def kernel(
-    text_ref, in_gain_ref, qw_ref, kvw_ref, ow_ref, q_gain_ref, k_gain_ref, gate_ref, vis_ref,
-    seg_ref, seg_img_ref, slot_ref, out_ref,
-    text, hid, hid_in, vis, wkv, wq, wo, wo_other, part, part_in, kv_rows, stage, kv_all, ctx, upd, upd_in,
+    text_ref, in_gain_hbm, qw_ref, kvw_ref, ow_ref, q_gain_hbm, k_gain_hbm, gate_ref, vis_ref,
+    seg_hbm, seg_img_hbm, slot_hbm, out_ref,
+    in_gain_ref, q_gain_ref, k_gain_ref, seg_ref, seg_img_ref, slot_ref, text, hid, hid_in, vis, wkv, wq, woa, wob, woa_other, wob_other, part, part_in, kv_rows, stage, kv_all, ctx, upd, upd_in,
     send_sem, recv_sem, local_sem,
 ):
     c = lax.axis_index("ctx")
@@ -56,15 +56,21 @@
         local.append(copy)
         return copy
 
-    get_text = fetch(text_ref, text)
+    get_text = [fetch(text_ref, text), fetch(in_gain_hbm, in_gain_ref)]
+    get_vis = [fetch(vis_ref.at[:, pl.ds(1024 * h, 1024)], vis.at[z, k, h]) for h in range(4)]
     get_own = [
-        fetch(vis_ref.at[:, pl.ds(0, 2048)], vis.at[z, k, 0]),
-        fetch(vis_ref.at[:, pl.ds(2048, 2048)], vis.at[z, k, 1]),
         fetch(kvw_ref.at[:, pl.ds(pl.multiple_of(z * 256 + k * 128, 128), 128)], wkv.at[c]),
         fetch(qw_ref, wq.at[y]),
-        fetch(ow_ref, wo.at[c]),
+        fetch(ow_ref.at[pl.ds(0, 128)], woa.at[x, y]),
+        fetch(ow_ref.at[pl.ds(128, 128)], wob.at[y, x]),
+        fetch(q_gain_hbm, q_gain_ref),
+        fetch(k_gain_hbm, k_gain_ref),
+        fetch(seg_hbm, seg_ref),
+        fetch(seg_img_hbm, seg_img_ref),
+        fetch(slot_hbm, slot_ref),
     ]
-    get_text.wait()
+    for copy in get_text:
+        copy.wait()
 
     @pl.loop(0, 8)
     def _(block):
@@ -75,37 +81,39 @@
         for b in range(32):
             hid[b % NX, b // NX // 4, b // NX % 4, rows, :] = values[:, b * 128:(b + 1) * 128]
 
-    for copy in get_own:
+    for copy in get_vis + get_own:
         copy.wait()
     pl.semaphore_wait(barrier, len(peers))
 
     vis_p, vis_m, vis_o = {}, {}, []
-    for h in (0, 1):
+    for h in range(4):
         vis_p[1, h] = send(vis.at[z, k, h], vis.at[z, k, h], to_z(1))
         vis_m[1, h] = send(vis.at[z, k, h], vis.at[z, k, h], to_z(-1))
     kv_y = {d: send(wkv.at[c], wkv.at[c], to_y(d)) for d in (1, -1, 2, -2, 3, -3, 4)}
     kv_x = [send(wkv.at[c], wkv.at[c], to_x(d)) for d in (1, -1, 2)]
-    for h in (0, 1):
-        vis_o.append(send(vis.at[z, k, h], vis.at[z, k, h], other))
+    vis_o.append(send(vis.at[z, k], vis.at[z, k], other))
     q_p, q_m = {}, {}
     q_p[1] = send(wq.at[y], wq.at[y], to_y(1))
     q_m[1] = send(wq.at[y], wq.at[y], to_y(-1))
     hid_x = {}
-    for d in (1, 3, 2):
-        hid_x[d] = send(hid.at[wrap(x + d, NX), k], hid_in.at[d - 1, k], to_x(d))
-    o_xp = send(wo.at[c], wo.at[c], to_x(1))
-    o_xm = send(wo.at[c], wo.at[c], to_x(-1))
+    a_p, a_m, b_p, b_m = {}, {}, {}, {}
+    a_p[1] = send(woa.at[x, y], woa.at[x, y], to_y(1))
+    a_m[1] = send(woa.at[x, y], woa.at[x, y], to_y(-1))
+    b_xp = send(wob.at[y, x], wob.at[y, x], to_x(1))
+    b_xm = send(wob.at[y, x], wob.at[y, x], to_x(-1))
 
     def vis_step(s):
-        for h in (0, 1):
+        for h in (0, 2, 1, 3):
             for ring, sign in ((vis_p, 1), (vis_m, -1)):
                 if (s, h) not in ring:
                     continue
                 ring[s, h].wait_recv()
-                block = vis.at[wrap(z - sign * s, NZ), k, h]
-                if s < 3 or (s == 3 and h == (0 if sign == 1 else 1)):
+                if s < 3 or (s == 3 and (h < 2) == (sign == 1)):
+                    block = vis.at[wrap(z - sign * s, NZ), k, h]
                     ring[s + 1, h] = send(block, block, to_z(sign))
-                vis_o.append(send(block, block, other))
+        for sign in ((1, -1) if s < 4 else (1,)):
+            block = vis.at[wrap(z - sign * s, NZ), k]
+            vis_o.append(send(block, block, other))
 
     def kv_step(s):
         for d in ((s, -s) if s < 4 else (4,)):
@@ -114,68 +122,69 @@
             for e in (1, -1, 2):
                 kv_x.append(send(block, block, to_x(e)))
 
-    def q_step(s):
-        for ring, sign in ((q_p, 1), (q_m, -1)):
-            ring[s].wait_recv()
-            block = wq.at[wrap(y - sign * s, NY)]
-            if s == 3:
-                block = block.at[pl.ds(0 if sign == 1 else 64, 64)]
-            if s < 4:
-                ring[s + 1] = send(block, block, to_y(sign))
-
-    o_p, o_m = {}, {}
-
-    def o_bundle(yy, first=0, count=NX):
-        return wo.at[pl.ds(yy * NX + first, count)]
-
-    def o_step(s):
-        for ring, sign in ((o_p, 1), (o_m, -1)):
+    def row_step(p, m, s, block, half):
+        for ring, sign in ((p, 1), (m, -1)):
             ring[s].wait_recv()
             yy = wrap(y - sign * s, NY)
-            block = o_bundle(yy)
-            if s == 3:
-                block = o_bundle(yy, 0 if sign == 1 else 2, 2)
             if s < 4:
-                ring[s + 1] = send(block, block, to_y(sign))
-                o_share(yy)
-        if s == 4:
-            o_share(wrap(y + 4, NY))
+                piece = half(yy, 0 if sign == 1 else 1) if s == 3 else block(yy)
+                ring[s + 1] = send(piece, piece, to_y(sign))
+
+    def q_step(s):
+        row_step(q_p, q_m, s, lambda yy: wq.at[yy], lambda yy, n: wq.at[yy, pl.ds(64 * n, 64)])
+
+    def a_step(s):
+        row_step(
+            a_p, a_m, s, lambda yy: woa.at[x, yy], lambda yy, n: woa.at[x, yy, pl.ds(64 * n, 64)]
+        )
 
     o_o = []
 
-    def o_share(yy):
-        o_o.append(send(wo.at[pl.ds(yy * NX + 2 * (1 - k), 2)], wo_other.at[yy], other))
+    def b_share(yy):
+        o_o.append(send(wob.at[yy, pl.ds(2 * (1 - k), 2)], wob_other.at[yy], other))
+
+    def b_step(s):
+        row_step(b_p, b_m, s, lambda yy: wob.at[yy], lambda yy, n: wob.at[yy, pl.ds(2 * n, 2)])
+        for d in ((s, -s) if s < 4 else (4,)):
+            b_share(wrap(y - d, NY))
 
     vis_step(1)
+    b_xp.wait_recv()
+    b_xm.wait_recv()
+    half = wob.at[y, wrap(x - 1, NX), pl.ds(0, 64)]
+    b_x2p = send(half, half, to_x(1))
+    half = wob.at[y, wrap(x + 1, NX), pl.ds(64, 64)]
+    b_x2m = send(half, half, to_x(-1))
     kv_step(1)
+    q_step(1)
+    a_step(1)
     vis_step(2)
     kv_step(2)
-    q_step(1)
-    o_xp.wait_recv()
-    o_xm.wait_recv()
-    half = wo.at[y * NX + wrap(x - 1, NX), pl.ds(0, 128)]
-    o_x2p = send(half, half, to_x(1))
-    half = wo.at[y * NX + wrap(x + 1, NX), pl.ds(128, 128)]
-    o_x2m = send(half, half, to_x(-1))
+    b_x2p.wait_recv()
+    b_x2m.wait_recv()
+    b_p[1] = send(wob.at[y], wob.at[y], to_y(1))
+    b_m[1] = send(wob.at[y], wob.at[y], to_y(-1))
+    b_share(y)
     kv_step(3)
     kv_step(4)
+    q_step(2)
+    a_step(2)
     vis_step(3)
-    q_step(2)
-    hid_o = {}
     for d in (1, 3, 2):
-        hid_x[d].wait_recv()
-        hid_o[d] = send(hid_in.at[d - 1, k], hid_in.at[d - 1, k], other)
+        hid_x[d] = send(hid.at[wrap(x + d, NX), k], hid_in.at[d - 1, k], to_x(d))
+    b_step(1)
+    q_step(3)
+    a_step(3)
     vis_step(4)
-    q_step(3)
     for copy in kv_x:
         copy.wait_recv()
     for copy in vis_o:
         copy.wait_recv()
 
     rows = jnp.zeros((256, 128), F32)
-    for h in (0, 1):
+    for h in range(4):
         rows += jnp.dot(
-            vis[:, :, h].reshape(256, 2048), wkv[16 * h:16 * (h + 1)].reshape(2048, 128),
+            vis[:, :, h].reshape(256, 1024), wkv[8 * h:8 * (h + 1)].reshape(1024, 128),
             preferred_element_type=F32,
         )
     mean_sq = jnp.mean(rows * rows, axis=-1, keepdims=True)
@@ -187,7 +196,7 @@
     def pick(block):
         tiles = []
         for s in range(8):
-            slot = slot_ref[seg_img_ref[block * 8 + s]]
+            slot = slot_ref[0, seg_img_ref[s % 2, block * 4 + s // 2]]
             tiles.append(kv_rows[slot])
         return jnp.concatenate(tiles, axis=0).astype(BF16)
 
@@ -201,11 +210,13 @@
         stage[n] = pick(yy * NX + xx)
         kv_a[n] = send(stage.at[n], kv_all.at[k, n], at(xx, yy, z, k))
 
-    o_x2p.wait_recv()
-    o_x2m.wait_recv()
-    o_p[1] = send(o_bundle(y), o_bundle(y), to_y(1))
-    o_m[1] = send(o_bundle(y), o_bundle(y), to_y(-1))
-    o_share(y)
+    b_step(2)
+    a_step(4)
+    a_x = {d: send(woa.at[x], woa.at[x], to_x(d)) for d in (1, -1)}
+    hid_o = {}
+    for d in (1, 3, 2):
+        hid_x[d].wait_recv()
+        hid_o[d] = send(hid_in.at[d - 1, k], hid_in.at[d - 1, k], other)
     q_step(4)
     for copy in hid_o.values():
         copy.wait_recv()
@@ -222,7 +233,7 @@
         else:
             part[d - 1] = product.astype(BF16)
             part_x[d] = send(part.at[d - 1], part_in.at[d - 1], to_x(-d))
-    o_step(1)
+    b_step(3)
     for d in (1, 3, 2):
         part_x[d].wait_recv()
         query += part_in[d - 1].astype(F32)
@@ -232,6 +243,13 @@
         mean_sq = jnp.mean(head * head, axis=-1, keepdims=True)
         heads.append((head * lax.rsqrt(mean_sq + EPS) * q_gain_ref[...]).astype(BF16))
 
+    for d in (1, -1):
+        a_x[d].wait_recv()
+    a_x2 = {}
+    for d in (1, -1):
+        piece = woa.at[wrap(x - d, NX), pl.ds(0 if d == 1 else 4, 4)]
+        a_x2[d] = send(piece, piece, to_x(d))
+    b_step(4)
     kv_o = []
     for dy in (1, 7, 2, 6, 3, 5, 4, 0):
         for dx in range(NX):
@@ -239,14 +257,14 @@
                 kv_a[dy * NX + dx].wait_recv()
         block = kv_all.at[k, pl.ds(dy * NX, NX)]
         kv_o.append(send(block, block, other))
-    o_step(2)
     for copy in kv_o:
         copy.wait_recv()
 
     keys = kv_all[0].reshape(2048, 128)
     values = kv_all[1].reshape(2048, 128)
     column = lax.broadcasted_iota(jnp.int32, (128, 2048), 1)
-    live = lax.rem(column, 64) // 16 == seg_ref[...] - 4 * c
+    segment = jnp.transpose(jnp.broadcast_to((seg_ref[...] - 4 * c).astype(F32), (128, 128)))
+    live = (lax.rem(column, 64) // 16).astype(F32) == segment[:, :1]
     for n in (0, 1):
         scores = lax.dot_general(
             heads[n], keys, (((1,), (1,)), ((), ())), preferred_element_type=F32
@@ -257,8 +275,10 @@
         acc = jnp.dot(weights.astype(BF16), values, preferred_element_type=F32)
         ctx[k, :, 128 * n:128 * (n + 1)] = (acc / total).astype(BF16)
     ctx_o = send(ctx.at[k], ctx.at[k], other)
-    o_step(3)
-    o_step(4)
+    for d in (1, -1):
+        a_x2[d].wait_recv()
+    for e in (0, 1):
+        o_o.append(send(woa.at[2 * (1 - k) + e], woa_other.at[e], other))
     for copy in o_o:
         copy.wait_recv()
     ctx_o.wait_recv()
@@ -268,8 +288,12 @@
     update = None
     for d in (4, 3, 5, 2, 6, 1, 7, 0):
         zz = wrap(z + d, NZ)
-        own_w = jnp.concatenate([wo[zz * NX + 2 * k + e] for e in (0, 1)], axis=1)
-        other_w = jnp.concatenate([wo_other[zz, e] for e in (0, 1)], axis=1)
+        own_a = jnp.concatenate([woa[2 * k + e, zz] for e in (0, 1)], axis=1)
+        own_b = jnp.concatenate([wob[zz, 2 * k + e] for e in (0, 1)], axis=1)
+        own_w = jnp.concatenate([own_a, own_b], axis=0)
+        other_a = jnp.concatenate([woa_other[e, zz] for e in (0, 1)], axis=1)
+        other_b = jnp.concatenate([wob_other[zz, e] for e in (0, 1)], axis=1)
+        other_w = jnp.concatenate([other_a, other_b], axis=0)
         product = jnp.dot(mine, own_w, preferred_element_type=F32)
         product += jnp.dot(theirs, other_w, preferred_element_type=F32)
         if d == 0:
@@ -293,21 +317,29 @@
 ):
     vmem = pl.BlockSpec(memory_space=pltpu.VMEM)
     smem = pl.BlockSpec(memory_space=pltpu.SMEM)
-    hbm = pl.BlockSpec(memory_space=pl.ANY)
+    hbm = pl.BlockSpec(memory_space=pltpu.HBM)
     return pl.pallas_call(
         kernel,
         out_shape=jax.ShapeDtypeStruct((128, 256), BF16),
-        in_specs=[hbm, vmem, hbm, hbm, hbm, vmem, vmem, smem, hbm, vmem, smem, smem],
+        in_specs=[hbm] * 7 + [smem] + [hbm] * 4,
         out_specs=vmem,
         scratch_shapes=[
+            pltpu.VMEM((1, 4096), F32),
+            pltpu.VMEM((1, 128), F32),
+            pltpu.VMEM((1, 128), F32),
+            pltpu.VMEM((1, 128), jnp.int32),
+            pltpu.SMEM((2, 128), jnp.int32),
+            pltpu.SMEM((1, 32), jnp.int32),
             pltpu.VMEM((128, 4096), BF16),
             pltpu.VMEM((4, 2, 4, 128, 128), BF16),
             pltpu.VMEM((3, 2, 4, 128, 128), BF16),
-            pltpu.VMEM((8, 2, 2, 16, 2048), BF16),
+            pltpu.VMEM((8, 2, 4, 16, 1024), BF16),
             pltpu.VMEM((32, 128, 128), BF16),
             pltpu.VMEM((8, 128, 256), BF16),
-            pltpu.VMEM((32, 256, 128), BF16),
-            pltpu.VMEM((8, 2, 256, 128), BF16),
+            pltpu.VMEM((4, 8, 128, 128), BF16),
+            pltpu.VMEM((8, 4, 128, 128), BF16),
+            pltpu.VMEM((2, 8, 128, 128), BF16),
+            pltpu.VMEM((8, 2, 128, 128), BF16),
             pltpu.VMEM((3, 128, 256), BF16),
             pltpu.VMEM((3, 128, 256), BF16),
             pltpu.VMEM((32, 8, 128), F32),
@@ -318,16 +350,16 @@
             pltpu.VMEM((7, 128, 256), BF16),
             pltpu.SemaphoreType.DMA((COPIES,)),
             pltpu.SemaphoreType.DMA((COPIES,)),
-            pltpu.SemaphoreType.DMA((8,)),
+            pltpu.SemaphoreType.DMA((32,)),
         ],
         compiler_params=pltpu.CompilerParams(
-            collective_id=0, has_side_effects=True, vmem_limit_bytes=48 * 2**20
+            collective_id=0, has_side_effects=True, vmem_limit_bytes=67 * 10**6
         ),
         cost_estimate=pl.CostEstimate(flops=2 * 10**9, bytes_accessed=4 * 10**6, transcendentals=600000),
     )(
         text, input_gain.reshape(1, -1), q_weight, kv_weight, o_weight, q_gain.reshape(1, -1),
-        k_gain.reshape(1, -1), attn_gate, vision.reshape(16, 4096), segment_ids.reshape(-1, 1),
-        seg_images.reshape(-1), image_slot,
+        k_gain.reshape(1, -1), attn_gate, vision.reshape(16, 4096), segment_ids.reshape(1, -1),
+        seg_images.T, image_slot.reshape(1, -1),
     )
 
 

time: 101 us -> 81.4 us (0.81)
  Pallas kernels: 93 us -> 79.1 us
  local copies, waits for them, and re-layouts: 6.68 us -> 1.47 us
    pallas_call x1, Pallas kernels: 93 us -> 79.1 us  [body(): pl.pallas_call(kernel, out_shape=jax.ShapeDtypeStruct((128, 256), BF16),...]
    unnamed x20 -> x1, local copies, waits for them, and re-layouts: 5.79 us -> 1.47 us
where the time goes in v2:
time: 81.4 us; the launch traced here: 81.3 us
  Pallas kernels  79.1 us (97%)
  local copies, waits for them, and re-layouts  1.47 us (2%)
    pallas_call x1, Pallas kernels, body(): pl.pallas_call(kernel, out_shape=jax.ShapeDtypeStruct((128, 256), BF16),...  79.1 us

profile of v2, /device:TPU:1, one launch (start us, length us, event | category | flops | bytes accessed | tf_op | source)
XLA Modules:
  0.0 81.3 jit_solution(11896657629402426646)
XLA Ops:
  0.7 79.1 %shard_map.118 = bf16[128,256]{1,0:T(8,128)(2,1)} custom-call(bf16[128,4096]{1,0:T(8,128)(2,1)} %text_ref.1, f32[1,4096]{1,0:T(1,128)} %bitcast.8, bf16[128,256]{1,0:T(8,128)(2,1)} %qw_ref.1, bf16[128,2048]{1,0:T(8,128)(2,1)} %kvw_ref.1, bf16[256,128]{1,0:T(8,128)(2,1)} %ow_ref.1, f32[1,128]{1,0:T(1,128)} %bitcast.10, f32[1,128]{1,0:T(1,128)} %bitcast.11, ...), custom_call_target="tpu_custom_call" | custom-call | flops 2000000000 | bytes 4000000 | tf_op jit(solution)/shard_map/pallas_call | solution.py:321
  79.8 1.5 %copy.15 = bf16[128,256]{1,0:T(8,128)(2,1)} copy(bf16[128,256]{1,0:T(8,128)(2,1)} %shard_map.118) | data formatting | bytes 131072

commit v3 on v2

v3 whole, which is shorter than its diff:
```python
import functools

import jax
import jax.numpy as jnp
from jax import lax
from jax.experimental import pallas as pl
from jax.experimental.pallas import tpu as pltpu
from jax.sharding import PartitionSpec as P

MESH = pl.DeviceIdType.MESH
EPS = 1e-05
NEG = -1e30
F32 = jnp.float32
BF16 = jnp.bfloat16
NX, NY, NZ = 4, 8, 8
COPIES = 192


def kernel(
    text_ref, in_gain_hbm, qw_ref, kvw_ref, ow_ref, q_gain_hbm, k_gain_hbm, gate_ref, vis_ref,
    seg_hbm, seg_img_hbm, slot_hbm, out_ref,
    in_gain_ref, q_gain_ref, k_gain_ref, seg_ref, seg_img_ref, slot_ref, text, hid, hid_in, vis, wkv, wq, woa, wob, woa_other, wob_other, part, part_in, kv_rows, stage, kv_all, ctx, upd, upd_in,
    send_sem, recv_sem, local_sem,
):
    c = lax.axis_index("ctx")
    i = lax.axis_index("img")
    x, y, z, k = lax.rem(c, NX), c // NX, i // 2, lax.rem(i, 2)
    wrap = lambda a, n: lax.rem(a + 2 * n, n)
    at = lambda xx, yy, zz, kk: (yy * NX + xx, zz * 2 + kk)
    to_x = lambda d: at(wrap(x + d, NX), y, z, k)
    to_y = lambda d: at(x, wrap(y + d, NY), z, k)
    to_z = lambda d: at(x, y, wrap(z + d, NZ), k)
    other = at(x, y, z, 1 - k)
    sent = []

    def send(src, dst, device):
        n = len(sent)
        copy = pltpu.make_async_remote_copy(
            src_ref=src, dst_ref=dst, send_sem=send_sem.at[n], recv_sem=recv_sem.at[n],
            device_id=device, device_id_type=MESH,
        )
        copy.start()
        sent.append(copy)
        return copy

    barrier = pltpu.get_barrier_semaphore()
    peers = [to_x(d) for d in (1, 2, 3)] + [to_y(d) for d in range(1, NY)]
    peers += [to_z(d) for d in range(1, NZ)] + [other]
    for peer in peers:
        pl.semaphore_signal(barrier, inc=1, device_id=peer, device_id_type=MESH)
    local = []

    def fetch(src, dst):
        copy = pltpu.make_async_copy(src, dst, local_sem.at[len(local)])
        copy.start()
        local.append(copy)
        return copy

    get_text = [fetch(text_ref, text), fetch(in_gain_hbm, in_gain_ref)]
    get_vis = [fetch(vis_ref.at[:, pl.ds(1024 * h, 1024)], vis.at[z, k, h]) for h in range(4)]
    get_own = [
        fetch(kvw_ref.at[:, pl.ds(pl.multiple_of(z * 256 + k * 128, 128), 128)], wkv.at[c]),
        fetch(qw_ref, wq.at[y]),
        fetch(ow_ref.at[pl.ds(0, 128)], woa.at[x, y]),
        fetch(ow_ref.at[pl.ds(128, 128)], wob.at[y, x]),
        fetch(q_gain_hbm, q_gain_ref),
        fetch(k_gain_hbm, k_gain_ref),
        fetch(seg_hbm, seg_ref),
        fetch(seg_img_hbm, seg_img_ref),
        fetch(slot_hbm, slot_ref),
    ]
    for copy in get_text:
        copy.wait()

    @pl.loop(0, 8)
    def _(block):
        rows = pl.ds(pl.multiple_of(block * 16, 16), 16)
        values = text[rows, :].astype(F32)
        mean_sq = jnp.mean(values * values, axis=-1, keepdims=True)
        values = (values * lax.rsqrt(mean_sq + EPS) * in_gain_ref[...]).astype(BF16)
        for b in range(32):
            hid[b % NX, b // NX // 4, b // NX % 4, rows, :] = values[:, b * 128:(b + 1) * 128]

    for copy in get_vis + get_own:
        copy.wait()
    pl.semaphore_wait(barrier, len(peers))

    vis_p, vis_m, vis_o = {}, {}, []
    kv_y, kv_x = {}, []
    q_p, q_m, a_p, a_m, b_p, b_m = {}, {}, {}, {}, {}, {}
    hid_x, hid_o, b_x, b_x2, a_x, a_x2, o_o = {}, {}, {}, {}, {}, {}, []
    part_x, kv_a, kv_o, heads, upd_z = {}, {}, [], [], {}
    query = []

    def vis_send():
        for h in range(4):
            vis_p[1, h] = send(vis.at[z, k, h], vis.at[z, k, h], to_z(1))
            vis_m[1, h] = send(vis.at[z, k, h], vis.at[z, k, h], to_z(-1))

    def vis_share():
        vis_o.append(send(vis.at[z, k], vis.at[z, k], other))

    def vis_step(s):
        for h in (0, 2, 1, 3):
            for ring, sign in ((vis_p, 1), (vis_m, -1)):
                if (s, h) not in ring:
                    continue
                ring[s, h].wait_recv()
                if s < 3 or (s == 3 and (h < 2) == (sign == 1)):
                    block = vis.at[wrap(z - sign * s, NZ), k, h]
                    ring[s + 1, h] = send(block, block, to_z(sign))
        for sign in ((1, -1) if s < 4 else (1,)):
            block = vis.at[wrap(z - sign * s, NZ), k]
            vis_o.append(send(block, block, other))

    def kv_send():
        for d in (1, -1, 2, -2, 3, -3, 4):
            kv_y[d] = send(wkv.at[c], wkv.at[c], to_y(d))

    def kv_send_x():
        kv_x.extend(send(wkv.at[c], wkv.at[c], to_x(d)) for d in (1, -1, 2))

    def kv_step(s):
        for d in ((s, -s) if s < 4 else (4,)):
            kv_y[d].wait_recv()
            block = wkv.at[wrap(y - d, NY) * NX + x]
            for e in (1, -1, 2):
                kv_x.append(send(block, block, to_x(e)))

    def row_send(p, m, block):
        p[1] = send(block, block, to_y(1))
        m[1] = send(block, block, to_y(-1))

    def row_step(p, m, s, block, half):
        for ring, sign in ((p, 1), (m, -1)):
            ring[s].wait_recv()
            yy = wrap(y - sign * s, NY)
            if s < 4:
                piece = half(yy, 0 if sign == 1 else 1) if s == 3 else block(yy)
                ring[s + 1] = send(piece, piece, to_y(sign))

    def q_send():
        row_send(q_p, q_m, wq.at[y])

    def q_step(s):
        row_step(q_p, q_m, s, lambda yy: wq.at[yy], lambda yy, n: wq.at[yy, pl.ds(64 * n, 64)])

    def a_send():
        row_send(a_p, a_m, woa.at[x, y])

    def a_step(s):
        row_step(
            a_p, a_m, s, lambda yy: woa.at[x, yy], lambda yy, n: woa.at[x, yy, pl.ds(64 * n, 64)]
        )

    def a_send_x():
        for d in (1, -1):
            a_x[d] = send(woa.at[x], woa.at[x], to_x(d))

    def a_step_x():
        for d in (1, -1):
            a_x[d].wait_recv()
        for d in (1, -1):
            piece = woa.at[wrap(x - d, NX), pl.ds(0 if d == 1 else 4, 4)]
            a_x2[d] = send(piece, piece, to_x(d))

    def a_share():
        for copy in a_x2.values():
            copy.wait_recv()
        for e in (0, 1):
            o_o.append(send(woa.at[2 * (1 - k) + e], woa_other.at[e], other))

    def b_share(yy):
        o_o.append(send(wob.at[yy, pl.ds(2 * (1 - k), 2)], wob_other.at[yy], other))

    def b_send_x():
        for d in (1, -1):
            b_x[d] = send(wob.at[y, x], wob.at[y, x], to_x(d))

    def b_step_x():
        for d in (1, -1):
            b_x[d].wait_recv()
        for d in (1, -1):
            half = wob.at[y, wrap(x - d, NX), pl.ds(0 if d == 1 else 64, 64)]
            b_x2[d] = send(half, half, to_x(d))

    def b_send():
        for copy in b_x2.values():
            copy.wait_recv()
        row_send(b_p, b_m, wob.at[y])
        b_share(y)

    def b_step(s):
        row_step(b_p, b_m, s, lambda yy: wob.at[yy], lambda yy, n: wob.at[yy, pl.ds(2 * n, 2)])
        for d in ((s, -s) if s < 4 else (4,)):
            b_share(wrap(y - d, NY))

    def hid_send():
        for d in (1, 3, 2):
            hid_x[d] = send(hid.at[wrap(x + d, NX), k], hid_in.at[d - 1, k], to_x(d))

    def hid_share():
        for d in (1, 3, 2):
            hid_x[d].wait_recv()
            hid_o[d] = send(hid_in.at[d - 1, k], hid_in.at[d - 1, k], other)

    def make_rows():
        for copy in kv_x + vis_o:
            copy.wait_recv()
        rows = jnp.zeros((256, 128), F32)
        for h in range(4):
            rows += jnp.dot(
                vis[:, :, h].reshape(256, 1024), wkv[8 * h:8 * (h + 1)].reshape(1024, 128),
                preferred_element_type=F32,
            )
        mean_sq = jnp.mean(rows * rows, axis=-1, keepdims=True)
        normed = rows * lax.rsqrt(mean_sq + EPS) * k_gain_ref[...]
        kv_rows[...] = jnp.where(k == 0, normed, rows).reshape(32, 8, 128)

    def pick(block):
        tiles = []
        for s in range(8):
            slot = slot_ref[0, seg_img_ref[s % 2, block * 4 + s // 2]]
            tiles.append(kv_rows[slot])
        return jnp.concatenate(tiles, axis=0).astype(BF16)

    def rows_send():
        for dy in (4, 3, 5, 2, 6, 1, 7, 0):
            for dx in (2, 1, 3, 0):
                n = dy * NX + dx
                if n == 0:
                    kv_all[k, 0] = pick(c)
                    continue
                xx, yy = wrap(x + dx, NX), wrap(y + dy, NY)
                stage[n] = pick(yy * NX + xx)
                kv_a[n] = send(stage.at[n], kv_all.at[k, n], at(xx, yy, z, k))

    def rows_share():
        for dy in (1, 7, 2, 6, 3, 5, 4, 0):
            for dx in range(NX):
                if (dx, dy) != (0, 0):
                    kv_a[dy * NX + dx].wait_recv()
            block = kv_all.at[k, pl.ds(dy * NX, NX)]
            kv_o.append(send(block, block, other))

    def part_send():
        for copy in hid_o.values():
            copy.wait_recv()
        wq_all = wq[...].reshape(1024, 256)
        for d in (1, 3, 2, 0):
            blocks = [
                (hid[x, b // 4, b % 4] if d == 0 else hid_in[d - 1, b // 4, b % 4]) for b in range(8)
            ]
            product = jnp.dot(jnp.concatenate(blocks, axis=1), wq_all, preferred_element_type=F32)
            if d == 0:
                query.append(product)
            else:
                part[d - 1] = product.astype(BF16)
                part_x[d] = send(part.at[d - 1], part_in.at[d - 1], to_x(-d))

    def make_query():
        total = query[0]
        for d in (1, 3, 2):
            part_x[d].wait_recv()
            total += part_in[d - 1].astype(F32)
        for n in (0, 1):
            head = total[:, 128 * n:128 * (n + 1)]
            mean_sq = jnp.mean(head * head, axis=-1, keepdims=True)
            heads.append((head * lax.rsqrt(mean_sq + EPS) * q_gain_ref[...]).astype(BF16))

    def attend():
        for copy in kv_o:
            copy.wait_recv()
        keys = kv_all[0].reshape(2048, 128)
        values = kv_all[1].reshape(2048, 128)
        column = lax.broadcasted_iota(jnp.int32, (128, 2048), 1)
        segment = jnp.transpose(jnp.broadcast_to((seg_ref[...] - 4 * c).astype(F32), (128, 128)))
        live = (lax.rem(column, 64) // 16).astype(F32) == segment[:, :1]
        for n in (0, 1):
            scores = lax.dot_general(
                heads[n], keys, (((1,), (1,)), ((), ())), preferred_element_type=F32
            ) * (128 ** -0.5)
            scores = jnp.where(live, scores, NEG)
            weights = jnp.exp(scores - jnp.max(scores, axis=-1, keepdims=True))
            total = jnp.sum(weights, axis=-1, keepdims=True)
            acc = jnp.dot(weights.astype(BF16), values, preferred_element_type=F32)
            ctx[k, :, 128 * n:128 * (n + 1)] = (acc / total).astype(BF16)
        o_o.append(send(ctx.at[k], ctx.at[k], other))

    def project():
        for copy in o_o:
            copy.wait_recv()
        mine, theirs = ctx[k], ctx[1 - k]

        def product(d):
            zz = wrap(z + d, NZ)
            own_a = jnp.concatenate([woa[2 * k + e, zz] for e in (0, 1)], axis=1)
            own_b = jnp.concatenate([wob[zz, 2 * k + e] for e in (0, 1)], axis=1)
            own_w = jnp.concatenate([own_a, own_b], axis=0)
            other_a = jnp.concatenate([woa_other[e, zz] for e in (0, 1)], axis=1)
            other_b = jnp.concatenate([wob_other[zz, e] for e in (0, 1)], axis=1)
            other_w = jnp.concatenate([other_a, other_b], axis=0)
            total = jnp.dot(mine, own_w, preferred_element_type=F32)
            return total + jnp.dot(theirs, other_w, preferred_element_type=F32)

        rows_of = {1: pl.ds(0, 64), -1: pl.ds(64, 64)}
        upd[3] = product(4).astype(BF16)
        for sign in (1, -1):
            upd_z[4 * sign] = send(upd.at[3, rows_of[sign]], upd_in.at[3, rows_of[sign]], to_z(2 * sign))
        for n, sign in ((4, 1), (5, -1)):
            upd[n] = product(3 * sign).astype(BF16)
            upd_z[3 * sign] = send(upd.at[n], upd_in.at[n], to_z(sign))
        for n, sign in ((0, 1), (1, -1)):
            upd[n] = product(sign).astype(BF16)
            upd_z[sign] = send(upd.at[n], upd_in.at[n], to_z(sign))
        two = {sign: product(2 * sign) for sign in (1, -1)}
        update = product(0).astype(BF16).astype(F32)
        for n, sign in ((2, 1), (6, -1)):
            upd_z[3 * sign].wait_recv()
            upd_z[4 * sign].wait_recv()
            total = two[sign] + upd_in[4 if sign == 1 else 5].astype(F32)
            upd[n] = total.astype(BF16)
            part_rows = rows_of[sign]
            first = 0 if sign == 1 else 64
            upd[n, part_rows] = (total[first:first + 64] + upd_in[3, part_rows].astype(F32)).astype(BF16)
            upd_z[2 * sign] = send(upd.at[n], upd_in.at[n], to_z(2 * sign))
        for n, d in ((0, 1), (1, -1), (2, 2), (6, -2)):
            upd_z[d].wait_recv()
            update += upd_in[n].astype(F32)
        own_text = text[:, pl.ds(pl.multiple_of(i * 256, 256), 256)].astype(F32)
        gate = jnp.tanh(jnp.full((1, 256), gate_ref[0], F32))
        out_ref[...] = (own_text + gate * update).astype(BF16)

    vis_send()
    kv_send()
    kv_send_x()
    vis_share()
    q_send()
    a_send()
    b_send_x()
    vis_step(1)
    b_step_x()
    kv_step(1)
    q_step(1)
    a_step(1)
    vis_step(2)
    kv_step(2)
    b_send()
    kv_step(3)
    kv_step(4)
    q_step(2)
    a_step(2)
    vis_step(3)
    hid_send()
    b_step(1)
    q_step(3)
    a_step(3)
    vis_step(4)
    make_rows()
    rows_send()
    b_step(2)
    a_step(4)
    a_send_x()
    hid_share()
    q_step(4)
    part_send()
    b_step(3)
    make_query()
    a_step_x()
    b_step(4)
    rows_share()
    attend()
    a_share()
    project()
    for copy in sent:
        copy.wait_send()


def body(
    text, input_gain, q_weight, kv_weight, o_weight, q_gain, k_gain, attn_gate, vision, segment_ids,
    seg_images, image_slot,
):
    vmem = pl.BlockSpec(memory_space=pltpu.VMEM)
    smem = pl.BlockSpec(memory_space=pltpu.SMEM)
    hbm = pl.BlockSpec(memory_space=pltpu.HBM)
    return pl.pallas_call(
        kernel,
        out_shape=jax.ShapeDtypeStruct((128, 256), BF16),
        in_specs=[hbm] * 7 + [smem] + [hbm] * 4,
        out_specs=vmem,
        scratch_shapes=[
            pltpu.VMEM((1, 4096), F32),
            pltpu.VMEM((1, 128), F32),
            pltpu.VMEM((1, 128), F32),
            pltpu.VMEM((1, 128), jnp.int32),
            pltpu.SMEM((2, 128), jnp.int32),
            pltpu.SMEM((1, 32), jnp.int32),
            pltpu.VMEM((128, 4096), BF16),
            pltpu.VMEM((4, 2, 4, 128, 128), BF16),
            pltpu.VMEM((3, 2, 4, 128, 128), BF16),
            pltpu.VMEM((8, 2, 4, 16, 1024), BF16),
            pltpu.VMEM((32, 128, 128), BF16),
            pltpu.VMEM((8, 128, 256), BF16),
            pltpu.VMEM((4, 8, 128, 128), BF16),
            pltpu.VMEM((8, 4, 128, 128), BF16),
            pltpu.VMEM((2, 8, 128, 128), BF16),
            pltpu.VMEM((8, 2, 128, 128), BF16),
            pltpu.VMEM((3, 128, 256), BF16),
            pltpu.VMEM((3, 128, 256), BF16),
            pltpu.VMEM((32, 8, 128), F32),
            pltpu.VMEM((32, 64, 128), BF16),
            pltpu.VMEM((2, 32, 64, 128), BF16),
            pltpu.VMEM((2, 128, 256), BF16),
            pltpu.VMEM((7, 128, 256), BF16),
            pltpu.VMEM((7, 128, 256), BF16),
            pltpu.SemaphoreType.DMA((COPIES,)),
            pltpu.SemaphoreType.DMA((COPIES,)),
            pltpu.SemaphoreType.DMA((32,)),
        ],
        compiler_params=pltpu.CompilerParams(
            collective_id=0, has_side_effects=True, vmem_limit_bytes=67 * 10**6
        ),
        cost_estimate=pl.CostEstimate(flops=2 * 10**9, bytes_accessed=4 * 10**6, transcendentals=600000),
    )(
        text, input_gain.reshape(1, -1), q_weight, kv_weight, o_weight, q_gain.reshape(1, -1),
        k_gain.reshape(1, -1), attn_gate, vision.reshape(16, 4096), segment_ids.reshape(1, -1),
        seg_images.T, image_slot.reshape(1, -1),
    )


def solution(mesh):
    return jax.shard_map(
        body,
        mesh=mesh,
        in_specs=(
            P("ctx", None), P(), P("ctx", "img"), P("ctx", None), P("img", "ctx"), P(), P(), P(),
            P("img", "ctx", None), P("ctx"), P(), P(),
        ),
        out_specs=P("ctx", "img"),
        check_vma=False,
    )
```

time: 81.4 us -> 76.7 us (0.942)
  Pallas kernels: 79.1 us -> 74.4 us
    pallas_call x1, Pallas kernels: 79.1 us -> 74.4 us  [body(): pl.pallas_call(kernel, out_shape=jax.ShapeDtypeStruct((128, 256), BF16),...]
where the time goes in v3:
time: 76.7 us; the launch traced here: 76.5 us
  Pallas kernels  74.4 us (97%)
  local copies, waits for them, and re-layouts  1.47 us (2%)
    pallas_call x1, Pallas kernels, body(): pl.pallas_call(kernel, out_shape=jax.ShapeDtypeStruct((128, 256), BF16),...  74.4 us

profile of v3, /device:TPU:1, one launch (start us, length us, event | category | flops | bytes accessed | tf_op | source)
XLA Modules:
  0.0 76.5 jit_solution(10706161351857161117)
XLA Ops:
  0.7 74.4 %shard_map.118 = bf16[128,256]{1,0:T(8,128)(2,1)} custom-call(bf16[128,4096]{1,0:T(8,128)(2,1)} %text_ref.1, f32[1,4096]{1,0:T(1,128)} %bitcast.8, bf16[128,256]{1,0:T(8,128)(2,1)} %qw_ref.1, bf16[128,2048]{1,0:T(8,128)(2,1)} %kvw_ref.1, bf16[256,128]{1,0:T(8,128)(2,1)} %ow_ref.1, f32[1,128]{1,0:T(1,128)} %bitcast.10, f32[1,128]{1,0:T(1,128)} %bitcast.11, ...), custom_call_target="tpu_custom_call" | custom-call | flops 2000000000 | bytes 4000000 | tf_op jit(solution)/shard_map/pallas_call | solution.py:386
  75.0 1.5 %copy.15 = bf16[128,256]{1,0:T(8,128)(2,1)} copy(bf16[128,256]{1,0:T(8,128)(2,1)} %shard_map.118) | data formatting | bytes 131072

commit v4 on v3

--- a/solution.py
+++ b/solution.py
@@ -157,18 +157,23 @@
         for d in (1, -1):
             a_x[d] = send(woa.at[x], woa.at[x], to_x(d))
 
+    near = jnp.where(x // 2 == 1 - k, lax.rem(x, 2), 1 - lax.rem(x, 2))
+
+    def a_pass(e):
+        o_o.append(send(woa.at[2 * (1 - k) + e], woa_other.at[e], other))
+
     def a_step_x():
         for d in (1, -1):
             a_x[d].wait_recv()
         for d in (1, -1):
             piece = woa.at[wrap(x - d, NX), pl.ds(0 if d == 1 else 4, 4)]
             a_x2[d] = send(piece, piece, to_x(d))
+        a_pass(near)
 
     def a_share():
         for copy in a_x2.values():
             copy.wait_recv()
-        for e in (0, 1):
-            o_o.append(send(woa.at[2 * (1 - k) + e], woa_other.at[e], other))
+        a_pass(1 - near)
 
     def b_share(yy):
         o_o.append(send(wob.at[yy, pl.ds(2 * (1 - k), 2)], wob_other.at[yy], other))
@@ -284,13 +289,13 @@
             weights = jnp.exp(scores - jnp.max(scores, axis=-1, keepdims=True))
             total = jnp.sum(weights, axis=-1, keepdims=True)
             acc = jnp.dot(weights.astype(BF16), values, preferred_element_type=F32)
-            ctx[k, :, 128 * n:128 * (n + 1)] = (acc / total).astype(BF16)
-        o_o.append(send(ctx.at[k], ctx.at[k], other))
+            ctx[k, n] = (acc / total).astype(BF16)
+            o_o.append(send(ctx.at[k, n], ctx.at[k, n], other))
 
     def project():
         for copy in o_o:
             copy.wait_recv()
-        mine, theirs = ctx[k], ctx[1 - k]
+        mine, theirs = (jnp.concatenate([ctx[m, n] for n in (0, 1)], axis=1) for m in (k, 1 - k))
 
         def product(d):
             zz = wrap(z + d, NZ)
@@ -358,18 +363,18 @@
     vis_step(4)
     make_rows()
     rows_send()
-    b_step(2)
     a_step(4)
     a_send_x()
+    b_step(2)
     hid_share()
     q_step(4)
     part_send()
+    a_step_x()
     b_step(3)
     make_query()
-    a_step_x()
-    b_step(4)
     rows_share()
     attend()
+    b_step(4)
     a_share()
     project()
     for copy in sent:
@@ -410,7 +415,7 @@
             pltpu.VMEM((32, 8, 128), F32),
             pltpu.VMEM((32, 64, 128), BF16),
             pltpu.VMEM((2, 32, 64, 128), BF16),
-            pltpu.VMEM((2, 128, 256), BF16),
+            pltpu.VMEM((2, 2, 128, 128), BF16),
             pltpu.VMEM((7, 128, 256), BF16),
             pltpu.VMEM((7, 128, 256), BF16),
             pltpu.SemaphoreType.DMA((COPIES,)),

time: 76.7 us -> 73.8 us (0.962)
  Pallas kernels: 74.4 us -> 71.1 us
    pallas_call x1, Pallas kernels: 74.4 us -> 71.1 us  [body(): pl.pallas_call(kernel, out_shape=jax.ShapeDtypeStruct((128, 256), BF16),...]
where the time goes in v4:
time: 73.8 us; the launch traced here: 73.2 us
  Pallas kernels  71.1 us (96%)
  local copies, waits for them, and re-layouts  1.47 us (2%)
    pallas_call x1, Pallas kernels, body(): pl.pallas_call(kernel, out_shape=jax.ShapeDtypeStruct((128, 256), BF16),...  71.1 us

profile of v4, /device:TPU:1, one launch (start us, length us, event | category | flops | bytes accessed | tf_op | source)
XLA Modules:
  0.0 73.2 jit_solution(12779637742641051781)
XLA Ops:
  0.7 71.1 %shard_map.118 = bf16[128,256]{1,0:T(8,128)(2,1)} custom-call(bf16[128,4096]{1,0:T(8,128)(2,1)} %text_ref.1, f32[1,4096]{1,0:T(1,128)} %bitcast.8, bf16[128,256]{1,0:T(8,128)(2,1)} %qw_ref.1, bf16[128,2048]{1,0:T(8,128)(2,1)} %kvw_ref.1, bf16[256,128]{1,0:T(8,128)(2,1)} %ow_ref.1, f32[1,128]{1,0:T(1,128)} %bitcast.10, f32[1,128]{1,0:T(1,128)} %bitcast.11, ...), custom_call_target="tpu_custom_call" | custom-call | flops 2000000000 | bytes 4000000 | tf_op jit(solution)/shard_map/pallas_call | solution.py:391
  71.8 1.5 %copy.15 = bf16[128,256]{1,0:T(8,128)(2,1)} copy(bf16[128,256]{1,0:T(8,128)(2,1)} %shard_map.118) | data formatting | bytes 131072

commit v5 on v4

--- a/solution.py
+++ b/solution.py
@@ -106,10 +106,13 @@
                 if (s, h) not in ring:
                     continue
                 ring[s, h].wait_recv()
+                if s == 4:
+                    block = vis.at[wrap(z + 4, NZ), k, h]
+                    vis_o.append(send(block, block, other))
                 if s < 3 or (s == 3 and (h < 2) == (sign == 1)):
                     block = vis.at[wrap(z - sign * s, NZ), k, h]
                     ring[s + 1, h] = send(block, block, to_z(sign))
-        for sign in ((1, -1) if s < 4 else (1,)):
+        for sign in ((1, -1) if s < 4 else ()):
             block = vis.at[wrap(z - sign * s, NZ), k]
             vis_o.append(send(block, block, other))
 
@@ -423,7 +426,7 @@
             pltpu.SemaphoreType.DMA((32,)),
         ],
         compiler_params=pltpu.CompilerParams(
-            collective_id=0, has_side_effects=True, vmem_limit_bytes=67 * 10**6
+            collective_id=0, has_side_effects=True, vmem_limit_bytes=56400000
         ),
         cost_estimate=pl.CostEstimate(flops=2 * 10**9, bytes_accessed=4 * 10**6, transcendentals=600000),
     )(

time: 73.8 us -> 73.9 us (level)
    unnamed x1 -> x13, local copies, waits for them, and re-layouts: 1.47 us -> 2.04 us
where the time goes in v5:
time: 73.9 us; the launch traced here: 73.2 us
  Pallas kernels  70.5 us (95%)
  local copies, waits for them, and re-layouts  2.04 us (3%)
    pallas_call x1, Pallas kernels, body(): pl.pallas_call(kernel, out_shape=jax.ShapeDtypeStruct((128, 256), BF16),...  70.5 us
    unnamed x13, local copies, waits for them, and re-layouts  2.04 us

profile of v5, /device:TPU:1, one launch (start us, length us, event | category | flops | bytes accessed | tf_op | source)
XLA Modules:
  0.0 73.2 jit_solution(8946947955410566215)
XLA Ops:
  0.7 0.0 copy-start.3
  0.7 0.0 copy-start.4
  0.7 0.0 copy-start.5
  0.7 0.0 copy-start.1
  0.7 0.0 copy-start.2
  0.7 0.6 copy-done.3
  1.3 0.0 copy-done.4
  1.3 0.0 copy-done.5
  1.3 0.0 copy-done.1
  1.4 0.0 copy-done.2
  1.4 0.0 copy-start
  1.4 0.7 copy-done
  2.1 70.5 %shard_map.118 = bf16[128,256]{1,0:T(8,128)(2,1)S(1)} custom-call(bf16[128,4096]{1,0:T(8,128)(2,1)} %text_ref.1, f32[1,4096]{1,0:T(1,128)S(1)} %bitcast.7, bf16[128,256]{1,0:T(8,128)(2,1)} %qw_ref.1, bf16[128,2048]{1,0:T(8,128)(2,1)} %kvw_ref.1, bf16[256,128]{1,0:T(8,128)(2,1)} %ow_ref.1, f32[1,128]{1,0:T(1,128)S(1)} %bitcast.9, f32[1,128]{1,0:T(1,128)S(1)} %bitcast.10, ...), custom_call_target="tpu_custom_call" | custom-call | flops 2000000000 | bytes 4000000 | tf_op jit(solution)/shard_map/pallas_call | solution.py:394
  72.6 0.6 copy.15
Async XLA Ops:
  0.7 0.7 copy-start.3
  0.7 0.7 copy-start.4
  0.7 0.7 copy-start.5
  0.7 0.7 copy-start.1
  0.7 0.7 copy-start.2
  1.4 0.7 copy-start
